TPU v7x, 32 devices: a whole 2x2x4 slice. The times are simulated.
32 devices in a mesh: groups: 2 (over y), wide: 4 (over z), dp: 4 (over x, core).
Axes of the slice: x: 2, y: 2, z: 4, core: 2. Of those that a mesh axis runs over, the one named last changes fastest.
Arguments:
- pair: bfloat16 [8, 256, 256, 128], P(('groups', 'dp'), 'wide'), parts along dimension 0, may hold values from -6 to 6
- lengths: int32 [8], P(('groups', 'dp')), parts along dimension 0, may hold values from 1 to 256, 640 in all
- gain_in: float32 [128], replicated, may hold values from 0.1 to 1.9
- tri_in: bfloat16 [4, 128, 128], replicated, may hold values from -0.5 to 0.5
- tri_gate: bfloat16 [128, 128], replicated, may hold values from -0.5 to 0.5
- gain_mid: float32 [128], replicated, may hold values from 0.1 to 1.9
- tri_out: bfloat16 [128, 128], replicated, may hold values from -0.5 to 0.5
- gain_att: float32 [128], replicated, may hold values from 0.1 to 1.9
- att_in: bfloat16 [4, 128, 128], replicated, may hold values from -0.5 to 0.5
- att_bias: bfloat16 [128, 4], replicated, may hold values from -16 to 16
- att_out: bfloat16 [128, 128], replicated, may hold values from -0.5 to 0.5
Outputs:
- updated_pair: bfloat16 [8, 256, 256, 128], P(('groups', 'dp'), 'wide'), parts along dimension 0
There are 2 independent parts, one for each index of `groups`. A program takes and returns all parts, laid end to end along the dimension named above; an argument that names none is the same for every part. Nothing has to cross between parts.
Inputs may be any that keep to these rules, and one draw needn't show every extreme that they name: `lengths`: each part has a crop of all 256 residues.
All inputs are finite; a program needn't handle non-finite values. No bound on the sum of `lengths` on one device may be relied on, other than what follows from the above.
Results may differ from a plain program's by a relative error of at most 0.023.
Values may be sent and summed in bfloat16 or wider, within the bound.
No kernel may reach another device: no remote copies, remote signals or barrier semaphores. Data moves between devices by JAX's collectives and lax.ppermute only.
A program may use at most 128 MiB of HBM per device.

v0:
```python
import jax
import jax.numpy as jnp
from jax import lax
from jax.sharding import PartitionSpec as P


def layer_norm(values, gain, axis):
    values = values.astype(jnp.float32)
    center = values - jnp.mean(values, axis=axis, keepdims=True)
    spread = jnp.mean(center * center, axis=axis, keepdims=True)
    shape = [1] * values.ndim
    shape[axis] = gain.shape[0]
    return center * lax.rsqrt(spread + 1e-05) * gain.reshape(shape)


def edge_operand(normed, weights, gate_index, proj_index, pair_mask):
    gate = jnp.einsum(
        "ikd,de->eik", normed, weights[gate_index], preferred_element_type=jnp.float32
    )
    proj = jnp.einsum(
        "ikd,de->eik", normed, weights[proj_index], preferred_element_type=jnp.float32
    )
    return (jax.nn.sigmoid(gate) * proj * pair_mask[None]).astype(jnp.bfloat16)


def row_update(block, normed, product, gain_mid, tri_out, tri_gate, gain_att, att_bias):
    mixed_in = layer_norm(product, gain_mid, 0).astype(jnp.bfloat16)
    update = jnp.einsum("cij,cd->ijd", mixed_in, tri_out, preferred_element_type=jnp.float32)
    gate = jax.nn.sigmoid(
        jnp.einsum("ijd,de->ije", normed, tri_gate, preferred_element_type=jnp.float32)
    )
    middle_rows = (block.astype(jnp.float32) + gate * update).astype(jnp.bfloat16)
    normed_rows = layer_norm(middle_rows, gain_att, 2).astype(jnp.bfloat16)
    bias_part = jnp.einsum(
        "ijc,ch->hij", normed_rows, att_bias, preferred_element_type=jnp.float32
    ).astype(jnp.bfloat16)
    return (middle_rows, bias_part)


def column_attention(normed, att_in, key_bias, heads):
    queries = jnp.einsum(
        "ijc,ce->jie", normed, att_in[0], preferred_element_type=jnp.float32
    ).astype(jnp.bfloat16)
    keys = jnp.einsum("ijc,ce->jie", normed, att_in[1], preferred_element_type=jnp.float32).astype(
        jnp.bfloat16
    )
    values = jnp.einsum(
        "ijc,ce->jie", normed, att_in[2], preferred_element_type=jnp.float32
    ).astype(jnp.bfloat16)
    gates = jax.nn.sigmoid(
        jnp.einsum("ijc,ce->jie", normed, att_in[3], preferred_element_type=jnp.float32)
    )
    count = queries.shape[1]
    width_all = queries.shape[2]
    depth = width_all // heads
    scale = depth ** (-0.5)

    def one_column(column):
        query, key, value, gate_col = column
        query = query.reshape(count, heads, depth)
        key = key.reshape(count, heads, depth)
        value = value.reshape(count, heads, depth)
        scores = (
            jnp.einsum("ihd,khd->hik", query, key, preferred_element_type=jnp.float32) * scale
            + key_bias
        )
        weights = jax.nn.softmax(scores, axis=-1).astype(jnp.bfloat16)
        mixed = jnp.einsum(
            "hik,khd->ihd", weights, value, preferred_element_type=jnp.float32
        ).reshape(count, width_all)
        return (gate_col * mixed).astype(jnp.bfloat16)

    return lax.map(one_column, (queries, keys, values, gates))


def body(
    pair, lengths, gain_in, tri_in, tri_gate, gain_mid, tri_out, gain_att, att_in, att_bias, att_out
):
    block = pair[0]
    rows = block.shape[0]
    count = block.shape[1]
    heads = att_bias.shape[1]
    first = lax.axis_index("wide") * rows
    mask = (jnp.arange(count) < lengths[0]).astype(jnp.float32)
    row_mask = lax.dynamic_slice_in_dim(mask, first, rows)
    pair_mask = row_mask[:, None] * mask[None, :]
    normed = layer_norm(block, gain_in, 2).astype(jnp.bfloat16)
    left = edge_operand(normed, tri_in, 0, 1, pair_mask)
    right = edge_operand(normed, tri_in, 2, 3, pair_mask)
    key_mask = ((mask - 1.0) * 1000000000.0)[None, None, :]
    left_ch, right_ch = (
        lax.all_to_all(left, "wide", split_axis=0, concat_axis=1, tiled=True),
        lax.all_to_all(right, "wide", split_axis=0, concat_axis=1, tiled=True),
    )
    product = jnp.einsum(
        "cik,cjk->cij", left_ch, right_ch, preferred_element_type=jnp.float32
    ).astype(jnp.bfloat16)
    product = lax.all_to_all(product, "wide", split_axis=1, concat_axis=0, tiled=True)
    middle_rows, bias_part = row_update(
        block, normed, product, gain_mid, tri_out, tri_gate, gain_att, att_bias
    )
    middle = lax.all_to_all(middle_rows, "wide", split_axis=1, concat_axis=0, tiled=True)
    table = lax.all_gather(bias_part, "wide", axis=1, tiled=True)
    normed_att = layer_norm(middle, gain_att, 2).astype(jnp.bfloat16)
    key_bias = jnp.swapaxes(table, 1, 2).astype(jnp.float32) + key_mask
    attended = column_attention(normed_att, att_in, key_bias, heads)
    result = jnp.einsum("jie,ec->ijc", attended, att_out, preferred_element_type=jnp.float32)
    finished = (middle.astype(jnp.float32) + result).astype(jnp.bfloat16)
    back = lax.all_to_all(finished, "wide", split_axis=0, concat_axis=1, tiled=True)
    return back[None]


def solution(mesh):
    in_specs = (
        P(("groups", "dp"), "wide", None, None),
        P(("groups", "dp")),
        P(),
        P(),
        P(),
        P(),
        P(),
        P(),
        P(),
        P(),
        P(),
    )
    out_specs = P(("groups", "dp"), "wide", None, None)
    return jax.shard_map(body, mesh=mesh, in_specs=in_specs, out_specs=out_specs, check_vma=False)
```

profile of v0, /device:TPU:0, one launch (start us, length us, event | category | flops | bytes accessed | tf_op | source)
XLA Modules:
  0.0 928.7 jit_solution(16951746255241277217)
XLA Ops:
  0.0 6.4 copy.89
  6.4 3.2 convert_reduce_fusion
  9.6 3.8 fusion.13
  14.3 3.8 fusion.65
  18.1 3.9 fusion.38
  22.0 4.4 copy.102
  26.3 6.5 all-to-all-start.1
  32.9 3.8 fusion.68
  36.7 3.9 fusion.37
  40.6 4.3 copy.96
  44.9 81.3 %all-to-all-done.1 = bf16[128,64,256]{2,1,0:T(8,128)(2,1)} async-done(((bf16[128,64,256]{2,1,0:T(8,128)(2,1)}), bf16[128,64,256]{2,1,0:T(8,128)(2,1)}, u32[]{:S(2)}, u32[]{:S(2)}) %all-to-all-start.1) | async-done | bytes 4194336 | tf_op jit(solution)/shard_map/all_to_all | solution.py:93
  126.3 4.9 all-to-all-start
  131.2 4.7 copy.103
  135.9 87.9 %all-to-all-done = bf16[128,64,256]{2,1,0:T(8,128)(2,1)} async-done(((bf16[128,64,256]{2,1,0:T(8,128)(2,1)}), bf16[128,64,256]{2,1,0:T(8,128)(2,1)}, u32[]{:S(2)}, u32[]{:S(2)}) %all-to-all-start) | async-done | bytes 4194336 | tf_op jit(solution)/shard_map/all_to_all | solution.py:92
  223.8 2.7 copy.97
  227.3 1.3 convolution_convert_fusion
  228.6 4.4 copy.104
  233.0 5.2 all-to-all-start.2
  238.2 6.9 fusion.30
  245.1 85.8 %all-to-all-done.2 = bf16[32,256,256]{2,0,1:T(8,128)(2,1)} async-done(((bf16[32,256,256]{2,0,1:T(8,128)(2,1)}), bf16[32,256,256]{2,0,1:T(8,128)(2,1)}, u32[]{:S(2)}, u32[]{:S(2)}) %all-to-all-start.2) | async-done | bytes 4194336 | tf_op jit(solution)/shard_map/all_to_all | solution.py:98
  330.8 3.2 fusion.28
  334.1 3.5 multiply_reduce_fusion.1
  337.6 3.2 convert_bitcast_fusion.2
  340.8 1.7 copy.105
  342.5 2.7 fusion.26
  345.3 7.5 convert_reduce_fusion.1
  352.8 6.6 copy.107
  359.4 5.1 all-to-all-start.3
  364.5 3.8 fusion.16
  368.3 3.6 fusion.55
  371.9 95.6 %all_gather.3 = bf16[4,256,256]{2,0,1:T(4,128)(2,1)S(1)} all-gather(bf16[4,64,256]{2,0,1:T(4,128)(2,1)S(1)} %fusion.55), channel_id=1, replica_groups=mesh['groups'=2,'wide'=4,'dp'=4] {'wide'}, dimensions={1}, use_global_device_ids=true | all-gather | bytes 655360 | tf_op jit(solution)/shard_map/all_gather | solution.py:103
  468.0 8.1 fusion.85
  476.1 2.3 fusion.27
  478.5 4.8 multiply_reduce_fusion
  483.4 7.4 multiply_convert_fusion.2
  490.8 1.3 copy.110
  492.2 7.2 divide_bitcast_fusion
  499.4 6.8 convert_bitcast_fusion.3
  506.1 6.7 convert_bitcast_fusion.4
  512.8 7.0 convert_bitcast_fusion.5
  519.9 299.5 %while.10 = (s32[]{:T(128)}, bf16[64,256,128]{1,2,0:T(8,128)(2,1)}, f32[64,256,128]{2,1,0:T(8,128)}, bf16[64,256,128]{2,1,0:T(8,128)(2,1)}, bf16[64,256,128]{2,1...) while((s32[]{:T(128)}, bf16[64,256,128]{1,2,0:T(8,128)(2,1)}, ...), condition=%wide.region_11.12_spmd, body=%wide.region_8.11_spmd.sunk | while | flops 35456512 | bytes 6169185 | solution.py:73
  532.3 0.9 constant_dynamic-slice_fusion.7
  536.9 0.9 constant_dynamic-slice_fusion.7
  819.3 8.4 copy.109
  827.7 1.3 fusion.23
  829.0 2.7 copy.122
  831.7 93.8 %all_to_all.69 = bf16[256,64,128]{2,1,0:T(8,128)(2,1)S(1)} all-to-all(bf16[256,64,128]{2,1,0:T(8,128)(2,1)S(1)} %copy.122), channel_id=1, replica_groups=mesh['groups'=2,'wide'=4,'dp'=4] {'wide'}, dimensions={0} | all-to-all | bytes 8388608 | tf_op jit(solution)/shard_map/all_to_all | solution.py:109
  925.5 3.0 copy.123
  (747 shorter events, 296.4 us)
Async XLA Ops:
  0.0 345.2 %copy-start = (bf16[128,128]{1,0:T(8,128)(2,1)S(1)}, bf16[128,128]{1,0:T(8,128)(2,1)}, u32[]{:S(2)}) copy-start(bf16[128,128]{1,0:T(8,128)(2,1)} %param.19) | copy-start | bytes 98308
  0.0 14.2 %copy-start.8 = (bf16[4,128,128]{2,1,0:T(8,128)(2,1)S(1)}, bf16[4,128,128]{2,1,0:T(8,128)(2,1)}, u32[]{:S(2)}) copy-start(bf16[4,128,128]{2,1,0:T(8,128)(2,1)} %param.16) | copy-start | bytes 393220
  0.0 14.2 %copy-start.11 = (f32[128]{0:T(128)S(1)}, f32[128]{0:T(128)}, u32[]{:S(2)}) copy-start(f32[128]{0:T(128)} %param.15) | copy-start | bytes 1540
  14.1 4.0 copy-start.2
  26.3 99.9 %all-to-all-start.1 = ((bf16[128,64,256]{2,1,0:T(8,128)(2,1)}), bf16[128,64,256]{2,1,0:T(8,128)(2,1)}, u32[]{:S(2)}, u32[]{:S(2)}) async-start(bf16[128,64,256]{2,1,0:T(8,128)(2,1)} %copy.102), calls=%async_computation.1 | async-start | bytes 8388608 | tf_op jit(solution)/shard_map/all_to_all | solution.py:93
  32.8 3.8 copy-start.3
  126.3 97.6 %all-to-all-start = ((bf16[128,64,256]{2,1,0:T(8,128)(2,1)}), bf16[128,64,256]{2,1,0:T(8,128)(2,1)}, u32[]{:S(2)}, u32[]{:S(2)}) async-start(bf16[128,64,256]{2,1,0:T(8,128)(2,1)} %copy.96), calls=%async_computation | async-start | bytes 8388608 | tf_op jit(solution)/shard_map/all_to_all | solution.py:92
  223.8 3.4 copy-start.5
  228.6 9.6 %copy-start.9 = (bf16[128,128]{1,0:T(8,128)(2,1)S(1)}, bf16[128,128]{1,0:T(8,128)(2,1)}, u32[]{:S(2)}) copy-start(bf16[128,128]{1,0:T(8,128)(2,1)} %param.17) | copy-start | bytes 98308
  233.0 97.8 %all-to-all-start.2 = ((bf16[32,256,256]{2,0,1:T(8,128)(2,1)}), bf16[32,256,256]{2,0,1:T(8,128)(2,1)}, u32[]{:S(2)}, u32[]{:S(2)}) async-start(bf16[32,256,256]{2,0,1:T(8,128)(2,1)} %copy.104), calls=%async_computation.2 | async-start | bytes 8388608 | tf_op jit(solution)/shard_map/all_to_all | solution.py:98
  340.8 1.7 copy-start.12
  342.5 2.8 copy-start.4
  359.4 8.9 copy-start.13
  359.4 8.9 copy-start.14
  359.4 108.6 %all-to-all-start.3 = ((bf16[64,256,128]{2,0,1:T(8,128)(2,1)}), bf16[64,256,128]{2,0,1:T(8,128)(2,1)}, u32[]{:S(2)}, u32[]{:S(2)}) async-start(bf16[64,256,128]{2,0,1:T(8,128)(2,1)} %copy.107), calls=%async_computation.3 | async-start | bytes 8388608 | tf_op jit(solution)/shard_map/all_to_all | solution.py:102
  483.4 8.7 copy-start.7
  819.3 8.4 copy-start.6
  819.3 8.4 copy-start.10
  829.0 99.5 %copy-start.1 = (bf16[128,128]{1,0:T(8,128)(2,1)S(1)}, bf16[128,128]{1,0:T(8,128)(2,1)}, u32[]{:S(2)}) copy-start(bf16[128,128]{1,0:T(8,128)(2,1)} %param.19) | copy-start | bytes 98308
where the time goes:
time: 944 us; the launch traced here: 929 us
  waiting for transfers between devices  255 us (27%)
  local copies, waits for them, and re-layouts  247 us (26%)
  blocking collectives  189 us (20%)
  matrix products  108 us (11%)
  other arithmetic  103 us (11%)
  starting transfers between devices  21.7 us (2%)
    dynamic_slice x448, local copies, waits for them, and re-layouts, column_attention(): return lax.map(one_column, (queries, keys, values, gates))  196 us
    all_gather x1, blocking collectives, body(): table = lax.all_gather(bias_part, 'wide', axis=1, tiled=True)  95.6 us
    all_to_all x1, blocking collectives, body(): lax.all_to_all(finished, 'wide', split_axis=0, concat_axis=1, tiled=True)  93.8 us
    all_to_all x1, waiting for transfers between devices, body(): lax.all_to_all(left, 'wide', split_axis=0, concat_axis=1, tiled=True)  87.9 us
    all_to_all x1, waiting for transfers between devices, body(): lax.all_to_all(product, 'wide', split_axis=1, concat_axis=0, tiled=True)  85.8 us
    all_to_all x1, waiting for transfers between devices, body(): lax.all_to_all(right, 'wide', split_axis=0, concat_axis=1, tiled=True)  81.3 us
    dynamic_update_slice x64, other arithmetic, column_attention(): return lax.map(one_column, (queries, keys, values, gates))  40.9 us
    dot_general x64, matrix products, one_column(): jnp.einsum('hik,khd->ihd', weights, value, preferred_element_type=jnp.flo...  22.5 us
  transfers between devices with their start and end apart: 4, of which 3 were waited for; matrix products, arithmetic and copies ran while one was open for 3% of the time, Pallas kernels for 0%

commit v1 on v0

--- a/solution.py
+++ b/solution.py
@@ -1,7 +1,21 @@
+import functools
+import math
+
 import jax
 import jax.numpy as jnp
 from jax import lax
+from jax.experimental import pallas as pl
+from jax.experimental.pallas import tpu as pltpu
 from jax.sharding import PartitionSpec as P
+
+EPS = 1e-05
+BLOCK = 16
+LANES = 128
+LOG2E = math.log2(math.e)
+VMEM = 40 * 1024 * 1024
+F32 = jnp.float32
+BF16 = jnp.bfloat16
+NT = (((1,), (1,)), ((), ()))
 
 
 def layer_norm(values, gain, axis):
@@ -10,7 +24,7 @@
     spread = jnp.mean(center * center, axis=axis, keepdims=True)
     shape = [1] * values.ndim
     shape[axis] = gain.shape[0]
-    return center * lax.rsqrt(spread + 1e-05) * gain.reshape(shape)
+    return center * lax.rsqrt(spread + EPS) * gain.reshape(shape)
 
 
 def edge_operand(normed, weights, gate_index, proj_index, pair_mask):
@@ -73,7 +87,7 @@
     return lax.map(one_column, (queries, keys, values, gates))
 
 
-def body(
+def general_body(
     pair, lengths, gain_in, tri_in, tri_gate, gain_mid, tri_out, gain_att, att_in, att_bias, att_out
 ):
     block = pair[0]
@@ -110,6 +124,407 @@
     return back[None]
 
 
+def norm_rows(values, ones, gain):
+    mean = jnp.dot(values.astype(BF16), ones, preferred_element_type=F32)
+    center = values - mean
+    spread = jnp.dot((center * center).astype(BF16), ones, preferred_element_type=F32)
+    return (center * lax.rsqrt(spread + EPS) * gain).astype(BF16)
+
+
+def operand_kernel(sides, first_index, scalars, x_ref, gain_ref, weight_ref, *refs):
+    outs, works = refs[:sides], refs[sides:]
+    count, chan = x_ref.shape[1], x_ref.shape[2]
+    length = scalars[0]
+    row0 = scalars[first_index] + pl.program_id(0) * BLOCK
+    ones = jnp.full((chan, chan), 1.0 / chan, BF16)
+    key_mask = (lax.broadcasted_iota(jnp.int32, (1, count), 1) < length).astype(F32)
+
+    def step(r, carry):
+        normed = norm_rows(x_ref[r].astype(F32), ones, gain_ref[...])
+        row_mask = key_mask * (row0 + r < length).astype(F32)
+        for side in range(sides):
+            gate = lax.dot_general(weight_ref[2 * side], normed, NT, preferred_element_type=F32)
+            proj = lax.dot_general(weight_ref[2 * side + 1], normed, NT, preferred_element_type=F32)
+            value = (jnp.tanh(gate) + 1.0) * proj * row_mask
+            for lane in range(count // LANES):
+                works[side][lane, pl.ds(r, chan, stride=BLOCK), :] = value[
+                    :, lane * LANES : (lane + 1) * LANES
+                ]
+        return carry
+
+    lax.fori_loop(0, BLOCK, step, 0, unroll=2)
+    for side in range(sides):
+        for lane in range(count // LANES):
+            outs[side][:, :, lane * LANES : (lane + 1) * LANES] = (
+                works[side][lane].reshape(chan, BLOCK, LANES).astype(BF16)
+            )
+
+
+def operands(x, scalars, first_index, gain, weights, sides):
+    rows, count, chan = x.shape
+    out = jax.ShapeDtypeStruct((chan, rows, count), BF16)
+    return pl.pallas_call(
+        functools.partial(operand_kernel, sides, first_index),
+        grid_spec=pltpu.PrefetchScalarGridSpec(
+            num_scalar_prefetch=1,
+            grid=(rows // BLOCK,),
+            in_specs=[
+                pl.BlockSpec((BLOCK, count, chan), lambda i, s: (i, 0, 0)),
+                pl.BlockSpec((1, chan), lambda i, s: (0, 0)),
+                pl.BlockSpec((2 * sides, chan, chan), lambda i, s: (0, 0, 0)),
+            ],
+            out_specs=[pl.BlockSpec((chan, BLOCK, count), lambda i, s: (0, i, 0))] * sides,
+            scratch_shapes=[pltpu.VMEM((count // LANES, chan * BLOCK, LANES), F32)] * sides,
+        ),
+        out_shape=[out] * sides,
+        compiler_params=pltpu.CompilerParams(vmem_limit_bytes=VMEM),
+        cost_estimate=pl.CostEstimate(
+            flops=2 * rows * count * chan * chan * (2 + 2 * sides),
+            bytes_accessed=2 * rows * count * chan * (1 + sides),
+            transcendentals=rows * count * chan * sides,
+        ),
+    )(scalars, x, gain, weights[: 2 * sides])
+
+
+def product_kernel(left_ref, mine_ref, partner_ref, out_ref):
+    for c in range(left_ref.shape[0]):
+        right = jnp.concatenate([mine_ref[c], partner_ref[c]], axis=0)
+        out_ref[c] = lax.dot_general(left_ref[c], right, NT, preferred_element_type=F32).astype(BF16)
+
+
+def products(left, mine, partner):
+    chan, rows, count = left.shape
+    own = mine.shape[1]
+    step = 8
+    return pl.pallas_call(
+        product_kernel,
+        grid=(chan // step,),
+        in_specs=[
+            pl.BlockSpec((step, rows, count), lambda i: (i, 0, 0)),
+            pl.BlockSpec((step, own, count), lambda i: (i, 0, 0)),
+            pl.BlockSpec((step, own, count), lambda i: (i, 0, 0)),
+        ],
+        out_specs=pl.BlockSpec((step, rows, 2 * own), lambda i: (i, 0, 0)),
+        out_shape=jax.ShapeDtypeStruct((chan, rows, 2 * own), BF16),
+        compiler_params=pltpu.CompilerParams(vmem_limit_bytes=VMEM),
+        cost_estimate=pl.CostEstimate(
+            flops=2 * chan * rows * count * 2 * own,
+            bytes_accessed=2 * chan * (rows * count + 2 * own * count + rows * 2 * own),
+            transcendentals=0,
+        ),
+    )(left, mine, partner)
+
+
+def update_kernel(
+    scalars,
+    prod_ref,
+    xm_ref,
+    xp_ref,
+    gain_in_ref,
+    gain_mid_ref,
+    gain_att_ref,
+    out_w_ref,
+    gate_w_ref,
+    bias_w_ref,
+    mine_ref,
+    partner_ref,
+    bias_ref,
+    work,
+    bias_work,
+):
+    chan, _, wide = prod_ref.shape
+    own = wide // 2
+    heads = bias_ref.shape[0]
+    pad = bias_w_ref.shape[0]
+    ones = jnp.full((chan, chan), 1.0 / chan, BF16)
+    work[...] = prod_ref[...].astype(F32).reshape(chan * BLOCK, wide)
+
+    def step(r, carry):
+        prod = work[pl.ds(r, chan, stride=BLOCK), :]
+        center = prod - jnp.mean(prod, axis=0, keepdims=True)
+        spread = jnp.mean(center * center, axis=0, keepdims=True)
+        mixed = (center * lax.rsqrt(spread + EPS) * gain_mid_ref[...]).astype(BF16)
+        update = jnp.dot(out_w_ref[...], mixed, preferred_element_type=F32).T
+        x = jnp.concatenate([xm_ref[r], xp_ref[r]], axis=0).astype(F32)
+        normed = norm_rows(x, ones, gain_in_ref[...])
+        gate = jnp.tanh(jnp.dot(normed, gate_w_ref[...], preferred_element_type=F32)) + 1.0
+        middle = (x + gate * update).astype(BF16)
+        mine_ref[r] = middle[:own]
+        partner_ref[r] = middle[own:]
+        normed_att = norm_rows(middle.astype(F32), ones, gain_att_ref[...])
+        bias_work[pl.ds(r, pad, stride=BLOCK), :] = lax.dot_general(
+            bias_w_ref[...], normed_att, NT, preferred_element_type=F32
+        )
+        return carry
+
+    lax.fori_loop(0, BLOCK, step, 0, unroll=2)
+    bias_ref[...] = bias_work[: heads * BLOCK, :].reshape(heads, BLOCK, wide).astype(BF16)
+
+
+def updates(prod, x, scalars, gain_in, gain_mid, gain_att, out_w, gate_w, bias_w, heads):
+    chan, rows, wide = prod.shape
+    own = wide // 2
+    pad = bias_w.shape[0]
+    full = lambda *shape: pl.BlockSpec(shape, lambda i, s: (0,) * len(shape))
+    return pl.pallas_call(
+        update_kernel,
+        grid_spec=pltpu.PrefetchScalarGridSpec(
+            num_scalar_prefetch=1,
+            grid=(rows // BLOCK,),
+            in_specs=[
+                pl.BlockSpec((chan, BLOCK, wide), lambda i, s: (0, i, 0)),
+                pl.BlockSpec((BLOCK, own, chan), lambda i, s: (i, s[1], 0)),
+                pl.BlockSpec((BLOCK, own, chan), lambda i, s: (i, s[2], 0)),
+                full(1, chan),
+                full(chan, 1),
+                full(1, chan),
+                full(chan, chan),
+                full(chan, chan),
+                full(pad, chan),
+            ],
+            out_specs=[
+                pl.BlockSpec((BLOCK, own, chan), lambda i, s: (i, 0, 0)),
+                pl.BlockSpec((BLOCK, own, chan), lambda i, s: (i, 0, 0)),
+                pl.BlockSpec((heads, BLOCK, wide), lambda i, s: (0, i, 0)),
+            ],
+            scratch_shapes=[
+                pltpu.VMEM((chan * BLOCK, wide), F32),
+                pltpu.VMEM((pad * BLOCK, wide), F32),
+            ],
+        ),
+        out_shape=[
+            jax.ShapeDtypeStruct((rows, own, chan), BF16),
+            jax.ShapeDtypeStruct((rows, own, chan), BF16),
+            jax.ShapeDtypeStruct((heads, rows, wide), BF16),
+        ],
+        compiler_params=pltpu.CompilerParams(vmem_limit_bytes=VMEM),
+        cost_estimate=pl.CostEstimate(
+            flops=2 * rows * wide * chan * chan * 7,
+            bytes_accessed=2 * rows * wide * chan * 3,
+            transcendentals=rows * wide * chan * 3,
+        ),
+    )(scalars, prod, x, x, gain_in, gain_mid, gain_att, out_w, gate_w, bias_w)
+
+
+def attention_kernel(
+    parts, heads, scalars, bias_own_ref, bias_oth_ref, gain_ref, wk_ref, wt_ref, wo_ref, *refs
+):
+    mine, recv = refs[:parts], refs[parts : 2 * parts]
+    outs = refs[2 * parts : 2 * parts + 4]
+    table, work, result = refs[2 * parts + 4 :]
+    count = table.shape[1]
+    chan = work.shape[1]
+    own = outs[0].shape[0]
+    depth = chan // heads
+    length = scalars[0]
+    ones = jnp.full((chan, chan), 1.0 / chan, BF16)
+    half = count // 2
+
+    @pl.when(scalars[11] == 0)
+    def _():
+        first = 0
+        for ref in mine:
+            size = ref.shape[0] * BLOCK
+            work[first : first + size, :] = ref[...].astype(F32).reshape(size, chan)
+            first += size
+
+    @pl.when(scalars[11] != 0)
+    def _():
+        first = 0
+        for ref in recv:
+            size = ref.shape[0] * BLOCK
+            work[first : first + size, :] = ref[...].astype(F32).reshape(size, chan)
+            first += size
+
+    for part in range(4):
+        place = lax.broadcasted_iota(jnp.int32, (own, half), 0) + scalars[3 + part] * own
+        masked = (jnp.where(place < length, 1.0, 0.0) - 1.0) * (1e9 * LOG2E)
+        turned = (part + 2) % 4
+        for h in range(heads):
+            rows = pl.ds(part * own, own)
+            table[h, rows, :half] = bias_own_ref[h, rows, :].astype(F32) * LOG2E + masked
+            table[h, rows, half:] = (
+                bias_oth_ref[h, pl.ds(turned * own, own), :].astype(F32) * LOG2E + masked
+            )
+
+    def column(b, carry):
+        x = work[pl.ds(b, count, stride=BLOCK), :]
+        normed = norm_rows(x, ones, gain_ref[...])
+        keys = jnp.dot(normed, wk_ref[...], preferred_element_type=F32).astype(BF16)
+        query = lax.dot_general(wt_ref[0], normed, NT, preferred_element_type=F32)
+        query = (query * (depth ** (-0.5) * LOG2E)).astype(BF16)
+        value = lax.dot_general(wt_ref[1], normed, NT, preferred_element_type=F32).astype(BF16)
+        gate = jnp.tanh(lax.dot_general(wt_ref[2], normed, NT, preferred_element_type=F32))
+        gate = 0.5 * gate + 0.5
+        attended = []
+        for h in range(heads):
+            pieces = []
+            if h > 0:
+                pieces.append(jnp.zeros((h * depth, count), BF16))
+            pieces.append(query[h * depth : (h + 1) * depth])
+            if h < heads - 1:
+                pieces.append(jnp.zeros(((heads - 1 - h) * depth, count), BF16))
+            alone = jnp.concatenate(pieces, axis=0)
+            scores = jnp.dot(keys, alone, preferred_element_type=F32) + table[h]
+            weights = jnp.exp2(scores - jnp.max(scores, axis=0, keepdims=True))
+            total = jnp.sum(weights, axis=0, keepdims=True)
+            mixed = jnp.dot(
+                value[h * depth : (h + 1) * depth],
+                weights.astype(BF16),
+                preferred_element_type=F32,
+            )
+            attended.append(mixed * (1.0 / total) * gate[h * depth : (h + 1) * depth])
+        attended = jnp.concatenate(attended, axis=0).astype(BF16)
+        update = jnp.dot(wo_ref[...], attended, preferred_element_type=F32).T
+        result[pl.ds(b, count, stride=BLOCK), :] = x + update
+        return carry
+
+    lax.fori_loop(0, BLOCK, column, 0)
+    for d in range(4):
+        rows = pl.ds(pl.multiple_of(scalars[7 + d] * (own * BLOCK), own * BLOCK), own * BLOCK)
+        outs[d][...] = result[rows, :].reshape(own, BLOCK, chan).astype(BF16)
+
+
+def attention(index, scalars, bias_own, bias_oth, gain, wk, wt, wo, mine, recv, heads):
+    own, chan = mine[0].shape[1], mine[0].shape[2]
+    count = 4 * own
+    full = lambda *shape: pl.BlockSpec(shape, lambda i, s: (0,) * len(shape))
+    pieces = [pl.BlockSpec((m.shape[0], BLOCK, chan), lambda i, s: (0, index, 0)) for m in mine]
+    return pl.pallas_call(
+        functools.partial(attention_kernel, len(mine), heads),
+        grid_spec=pltpu.PrefetchScalarGridSpec(
+            num_scalar_prefetch=1,
+            grid=(1,),
+            in_specs=[
+                full(heads, count, count // 2),
+                full(heads, count, count // 2),
+                full(1, chan),
+                full(chan, chan),
+                full(3, chan, chan),
+                full(chan, chan),
+            ]
+            + pieces
+            + pieces,
+            out_specs=[full(own, BLOCK, chan)] * 4,
+            scratch_shapes=[
+                pltpu.VMEM((heads, count, count), F32),
+                pltpu.VMEM((count * BLOCK, chan), F32),
+                pltpu.VMEM((count * BLOCK, chan), F32),
+            ],
+        ),
+        out_shape=[jax.ShapeDtypeStruct((own, BLOCK, chan), BF16)] * 4,
+        compiler_params=pltpu.CompilerParams(vmem_limit_bytes=VMEM),
+        cost_estimate=pl.CostEstimate(
+            flops=2 * BLOCK * (count * chan * chan * 7 + 2 * heads * count * count * chan),
+            bytes_accessed=2 * count * BLOCK * chan * 3,
+            transcendentals=BLOCK * heads * count * count,
+        ),
+    )(scalars, bias_own, bias_oth, gain, wk, wt, wo, *mine, *recv)
+
+
+def line_body(
+    pair, lengths, gain_in, tri_in, tri_gate, gain_mid, tri_out, gain_att, att_in, att_bias, att_out
+):
+    own_rows = pair[0]
+    own, count, chan = own_rows.shape
+    heads = att_bias.shape[1]
+    z = lax.axis_index("wide")
+    inner = jnp.where(z < 2, 1, 2)
+    partner = inner ^ 1
+    other_in = 3 - inner
+    other_out = other_in ^ 1
+    order = jnp.stack([inner, partner, other_in, other_out])
+    outer = ((z == 0) | (z == 3)).astype(jnp.int32)
+    place = jnp.stack([jnp.argmax(order == (z + d) % 4) for d in range(4)])
+    half_rows = own // 2
+    firsts = order * own
+    scalars = jnp.concatenate(
+        [
+            lengths[:1],
+            jnp.stack([inner, partner]),
+            order,
+            place,
+            jnp.stack([outer]),
+            firsts,
+            firsts + half_rows,
+        ]
+    ).astype(jnp.int32)
+
+    to_inner = [(0, 1), (3, 2)]
+    to_outer = [(1, 0), (2, 3)]
+    middle_link = [(1, 2), (2, 1)]
+    send = lambda v, pairs: lax.ppermute(v, "wide", pairs)
+
+    partner_parts = [send(own_rows[:half_rows], to_inner), send(own_rows[half_rows:], to_inner)]
+    rows_oi = send(own_rows, middle_link)
+    rows_oo = [send(v, middle_link) for v in partner_parts]
+
+    tri_w = (jnp.swapaxes(tri_in, 1, 2).astype(F32) * 0.5).astype(BF16)
+    gain_row = gain_in.reshape(1, chan)
+    left_own, right_own = operands(own_rows, scalars, 12, gain_row, tri_w, 2)
+    chunks = [(own_rows, left_own)]
+    rights = []
+    rows_p = jnp.concatenate(partner_parts, axis=0)
+    left_p, right_p = operands(rows_p, scalars, 13, gain_row, tri_w, 2)
+    chunks.append((rows_p, left_p))
+    chunks.append((rows_oi, operands(rows_oi, scalars, 14, gain_row, tri_w, 1)[0]))
+    chunks.append((rows_oo[0], operands(rows_oo[0], scalars, 15, gain_row, tri_w, 1)[0]))
+    chunks.append((rows_oo[1], operands(rows_oo[1], scalars, 19, gain_row, tri_w, 1)[0]))
+
+    out_w = (tri_out.astype(F32) * 0.5).astype(BF16).T
+    gate_w = (tri_gate.astype(F32) * 0.5).astype(BF16)
+    bias_w = jnp.zeros((8, chan), BF16).at[:heads].set(att_bias.T)
+    mine, recv, biases = [], [], []
+    for rows, left in chunks:
+        prod = products(left, right_own, right_p)
+        kept, sent, bias = updates(
+            prod,
+            rows,
+            scalars,
+            gain_row,
+            gain_mid.reshape(chan, 1),
+            gain_att.reshape(1, chan),
+            out_w,
+            gate_w,
+            bias_w,
+            heads,
+        )
+        mine.append(kept)
+        recv.append(send(sent, to_outer))
+        biases.append(bias)
+
+    bias_own = jnp.concatenate(biases, axis=1)
+    bias_oth = send(bias_own, middle_link)
+    got_own, got_oth = send(bias_own, to_outer), send(bias_oth, to_outer)
+    bias_own = jnp.where(outer == 1, got_own, bias_own)
+    bias_oth = jnp.where(outer == 1, got_oth, bias_oth)
+
+    att_t = jnp.swapaxes(att_in, 1, 2)
+    wt = jnp.stack([att_t[0], att_t[2], (att_t[3].astype(F32) * 0.5).astype(BF16)])
+    output = jnp.zeros((own, count, chan), BF16)
+    for index in range(own // BLOCK):
+        outs = attention(
+            index,
+            scalars,
+            bias_own,
+            bias_oth,
+            gain_att.reshape(1, chan),
+            att_in[1],
+            wt,
+            att_out.T,
+            mine,
+            recv,
+            heads,
+        )
+        for d in range(4):
+            piece = outs[d]
+            if d > 0:
+                piece = send(piece, [(i, (i + d) % 4) for i in range(4)])
+            source = (z - d) % 4
+            output = lax.dynamic_update_slice(output, piece, (0, source * own + index * BLOCK, 0))
+    return output[None]
+
+
 def solution(mesh):
     in_specs = (
         P(("groups", "dp"), "wide", None, None),
@@ -125,4 +540,5 @@
         P(),
     )
     out_specs = P(("groups", "dp"), "wide", None, None)
+    body = line_body if mesh.shape["wide"] == 4 else general_body
     return jax.shard_map(body, mesh=mesh, in_specs=in_specs, out_specs=out_specs, check_vma=False)

time: 944 us -> 785 us (0.83); the launches traced: 929 us -> 783 us
  Pallas kernels: 0 us -> 482 us
  local copies, waits for them, and re-layouts: 247 us -> 41.4 us
  blocking collectives: 189 us -> 0 us
  matrix products: 108 us -> 0 us
  other arithmetic: 103 us -> 5.05 us
  waiting for transfers between devices: 255 us -> 206 us
  starting transfers between devices: 21.7 us -> 46.6 us
    pallas_call x0 -> x19, Pallas kernels: none -> 482 us  [the longest x5 191 us: updates(): pl.pallas_call(update_kernel, grid_spec=pltpu.PrefetchScalarGridSpec(num_...]
    all_to_all x4 -> x0, waiting for transfers between devices: 255 us -> none  [the longest x1 87.9 us: body(): lax.all_to_all(left, 'wide', split_axis=0, concat_axis=1, tiled=True)]
    ppermute x0 -> x25, waiting for transfers between devices: none -> 206 us  [line_body(): send = lambda v, pairs: lax.ppermute(v, 'wide', pairs)]
    dynamic_slice x449 -> x0, local copies, waits for them, and re-layouts: 196 us -> none  [the longest x448 196 us: column_attention(): return lax.map(one_column, (queries, keys, values, gates))]
    dot_general x141 -> x0, matrix products: 108 us -> none  [the longest x64 22.5 us: one_column(): jnp.einsum('hik,khd->ihd', weights, value, preferred_element_type=jnp.flo...]
    all_gather x1 -> x0, blocking collectives: 95.6 us -> none  [body(): table = lax.all_gather(bias_part, 'wide', axis=1, tiled=True)]
    all_to_all x1 -> x0, blocking collectives: 93.8 us -> none  [body(): lax.all_to_all(finished, 'wide', split_axis=0, concat_axis=1, tiled=True)]
    ppermute x0 -> x25, starting transfers between devices: none -> 46.6 us  [line_body(): send = lambda v, pairs: lax.ppermute(v, 'wide', pairs)]
  transfers between devices with their start and end apart: 4 -> 25, of which waited for: 3 -> 9; matrix products, arithmetic and copies ran while one was open for 3% -> 2% of each run, Pallas kernels for 0% -> 43%
where the time goes in v1:
time: 785 us; the launch traced here: 783 us
  Pallas kernels  482 us (61%)
  waiting for transfers between devices  206 us (26%)
  starting transfers between devices  46.6 us (6%)
  local copies, waits for them, and re-layouts  41.4 us (5%)
    ppermute x25, waiting for transfers between devices, line_body(): send = lambda v, pairs: lax.ppermute(v, 'wide', pairs)  206 us
    pallas_call x5, Pallas kernels, updates(): pl.pallas_call(update_kernel, grid_spec=pltpu.PrefetchScalarGridSpec(num_...  191 us
    pallas_call x5, Pallas kernels, operands(): pl.pallas_call(functools.partial(operand_kernel, sides, first_index), gri...  134 us
    pallas_call x4, Pallas kernels, attention(): pl.pallas_call(functools.partial(attention_kernel, len(mine), heads), gri...  116 us
    ppermute x25, starting transfers between devices, line_body(): send = lambda v, pairs: lax.ppermute(v, 'wide', pairs)  46.6 us
    pallas_call x5, Pallas kernels, products(): pl.pallas_call(product_kernel, grid=(chan // step,), in_specs=[pl.BlockSp...  40.6 us
    unnamed x82, local copies, waits for them, and re-layouts  29.6 us
  transfers between devices with their start and end apart: 25, of which 9 were waited for; matrix products, arithmetic and copies ran while one was open for 2% of the time, Pallas kernels for 43%

profile of v1, /device:TPU:0, one launch (start us, length us, event | category | flops | bytes accessed | tf_op | source)
XLA Modules:
  0.0 782.8 jit_solution(1086236472594329665)
XLA Ops:
  0.0 4.0 slice_bitcast_fusion
  4.0 6.3 collective-permute-start
  10.3 2.6 collective-permute-start.2
  12.9 2.6 collective-permute-start.1
  17.8 37.2 %collective-permute-done = bf16[32,256,128]{2,1,0:T(8,128)(2,1)} collective-permute-done((bf16[32,256,128]{2,1,0:T(8,128)(2,1)S(1)}, bf16[32,256,128]{2,1,0:T(8,128)(2,1)}, u32[]{:S(2)}, u32[]{:S(2)}) %collective-permute-start) | collective-permute-done | bytes 2097184 | tf_op jit(solution)/shard_map/ppermute | solution.py:456
  56.7 42.2 %collective-permute-done.1 = bf16[32,256,128]{2,1,0:T(8,128)(2,1)} collective-permute-done((bf16[32,256,128]{2,1,0:T(8,128)(2,1)}, bf16[32,256,128]{2,1,0:T(8,128)(2,1)}, u32[]{:S(2)}, u32[]{:S(2)}) %collective-permute-start.1) | collective-permute-done | bytes 2097184 | tf_op jit(solution)/shard_map/ppermute | solution.py:456
  98.9 2.0 collective-permute-start.4
  101.9 2.6 concatenate.12.scalars
  104.5 36.5 %shard_map.109 = (bf16[128,64,256]{2,1,0:T(8,128)(2,1)S(1)}, bf16[128,64,256]{2,1,0:T(8,128)(2,1)S(1)}) custom-call(s32[20]{0:T(128)S(1)} %concatenate.12.scalars, bf16[64,256,128]{2,1,0:T(8,128)(2,1)} %bitcast.9.x_ref.xm_ref.xp_ref, f32[1,128]{1,0:T(1,128)S(1)} %bitcast.58, bf16[4,128,128]{2,1,0:T(8,128)(2,1)S(1)} %fusion.weight_ref), custom_call_target="tpu_custom_call" | custom-call | flops 3221225472 | bytes 12582912 | tf_op jit(solution)/shard_map/pallas_call | solution.py:166
  141.0 2.0 copy-done.5
  143.0 1.7 constant_dynamic-update-slice_fusion.1
  144.7 1.9 constant_dynamic-update-slice_fusion.x_ref.xm_ref.xp_ref
  146.7 35.2 %shard_map.110 = (bf16[128,64,256]{2,1,0:T(8,128)(2,1)S(1)}, bf16[128,64,256]{2,1,0:T(8,128)(2,1)S(1)}) custom-call(s32[20]{0:T(128)S(1)} %concatenate.12.scalars, bf16[64,256,128]{2,1,0:T(8,128)(2,1)S(1)} %constant_dynamic-update-slice_fusion.x_ref.xm_ref.xp_ref, f32[1,128]{1,0:T(1,128)S(1)} %bitcast.59, bf16[4,128,128]{2,1,0:T(8,128)(2,1)S(1)} %fusion.weight_ref), custom_call_target="tpu_custom_call" | custom-call | flops 3221225472 | bytes 12582912 | tf_op jit(solution)/shard_map/pallas_call | solution.py:166
  181.9 2.0 copy-done
  183.9 2.0 copy-done.7
  185.9 2.2 copy-done.6
  188.1 10.5 %shard_map.111.prod_ref = bf16[128,64,128]{2,1,0:T(8,128)(2,1)S(1)} custom-call(bf16[128,64,256]{2,1,0:T(8,128)(2,1)S(1)} %copy-done.6, bf16[128,64,256]{2,1,0:T(8,128)(2,1)S(1)} %get-tuple-element.61.mine_ref, bf16[128,64,256]{2,1,0:T(8,128)(2,1)} %copy-done), custom_call_target="tpu_custom_call" | custom-call | flops 536870912 | bytes 14680064 | tf_op jit(solution)/shard_map/pallas_call | solution.py:199
  200.0 2.2 copy-done.8
  202.2 10.6 %shard_map.113.prod_ref = bf16[128,64,128]{2,1,0:T(8,128)(2,1)S(1)} custom-call(bf16[128,64,256]{2,1,0:T(8,128)(2,1)S(1)} %copy-done.8, bf16[128,64,256]{2,1,0:T(8,128)(2,1)S(1)} %get-tuple-element.61.mine_ref, bf16[128,64,256]{2,1,0:T(8,128)(2,1)} %copy-done), custom_call_target="tpu_custom_call" | custom-call | flops 536870912 | bytes 14680064 | tf_op jit(solution)/shard_map/pallas_call | solution.py:199
  212.7 1.6 copy-done.4
  214.3 47.9 %shard_map.112 = (bf16[64,64,128]{2,1,0:T(8,128)(2,1)S(1)}, bf16[64,64,128]{2,1,0:T(8,128)(2,1)S(1)}, bf16[4,64,128]{2,1,0:T(8,128)(2,1)S(1)}) custom-call(s32[20]{0:T(128)S(1)} %concatenate.12.scalars, bf16[128,64,128]{2,1,0:T(8,128)(2,1)S(1)} %copy-done.4, bf16[64,256,128]{2,1,0:T(8,128)(2,1)} %bitcast.9.x_ref.xm_ref.xp_ref, ...), custom_call_target="tpu_custom_call" | custom-call | flops 1879048192 | bytes 6291456 | tf_op jit(solution)/shard_map/pallas_call | solution.py:269
  263.9 47.0 %shard_map.114 = (bf16[64,64,128]{2,1,0:T(8,128)(2,1)S(1)}, bf16[64,64,128]{2,1,0:T(8,128)(2,1)S(1)}, bf16[4,64,128]{2,1,0:T(8,128)(2,1)S(1)}) custom-call(s32[20]{0:T(128)S(1)} %concatenate.12.scalars, bf16[128,64,128]{2,1,0:T(8,128)(2,1)S(1)} %shard_map.113.prod_ref, bf16[64,256,128]{2,1,0:T(8,128)(2,1)S(1)} %constant_dynamic-update-slice_fusion.x_ref.xm_ref.xp_ref, ...), custom_call_target="tpu_custom_call" | custom-call | flops 1879048192 | bytes 6291456 | tf_op jit(solution)/shard_map/pallas_call | solution.py:269
  312.9 15.1 %shard_map.118.left_ref = bf16[128,32,256]{2,1,0:T(8,128)(2,1)S(1)} custom-call(s32[20]{0:T(128)S(1)} %concatenate.12.scalars, bf16[32,256,128]{2,1,0:T(8,128)(2,1)S(1)} %collective-permute-done.3.x_ref.xm_ref.xp_ref, f32[1,128]{1,0:T(1,128)S(1)} %bitcast.62, bf16[2,128,128]{2,1,0:T(8,128)(2,1)S(1)} %slice.57.weight_ref), custom_call_target="tpu_custom_call" | custom-call | flops 1073741824 | bytes 4194304 | tf_op jit(solution)/shard_map/pallas_call | solution.py:166
  328.1 4.5 shard_map.119.prod_ref
  332.6 30.9 %shard_map.115.left_ref = bf16[128,64,256]{2,1,0:T(8,128)(2,1)S(1)} custom-call(s32[20]{0:T(128)S(1)} %concatenate.12.scalars, bf16[64,256,128]{2,1,0:T(8,128)(2,1)} %collective-permute-done.2.x_ref.xm_ref.xp_ref, f32[1,128]{1,0:T(1,128)S(1)} %bitcast.63, bf16[2,128,128]{2,1,0:T(8,128)(2,1)S(1)} %slice.57.weight_ref), custom_call_target="tpu_custom_call" | custom-call | flops 2147483648 | bytes 8388608 | tf_op jit(solution)/shard_map/pallas_call | solution.py:166
  363.6 10.5 %shard_map.116.prod_ref = bf16[128,64,128]{2,1,0:T(8,128)(2,1)S(1)} custom-call(bf16[128,64,256]{2,1,0:T(8,128)(2,1)S(1)} %shard_map.115.left_ref, bf16[128,64,256]{2,1,0:T(8,128)(2,1)S(1)} %get-tuple-element.61.mine_ref, bf16[128,64,256]{2,1,0:T(8,128)(2,1)} %copy-done), custom_call_target="tpu_custom_call" | custom-call | flops 536870912 | bytes 14680064 | tf_op jit(solution)/shard_map/pallas_call | solution.py:199
  374.1 16.7 %shard_map.121.left_ref = bf16[128,32,256]{2,1,0:T(8,128)(2,1)S(1)} custom-call(s32[20]{0:T(128)S(1)} %concatenate.12.scalars, bf16[32,256,128]{2,1,0:T(8,128)(2,1)} %collective-permute-done.4.x_ref.xm_ref.xp_ref, f32[1,128]{1,0:T(1,128)S(1)} %bitcast.64, bf16[2,128,128]{2,1,0:T(8,128)(2,1)S(1)} %slice.57.weight_ref), custom_call_target="tpu_custom_call" | custom-call | flops 1073741824 | bytes 4194304 | tf_op jit(solution)/shard_map/pallas_call | solution.py:166
  390.8 4.5 shard_map.122.prod_ref
  395.3 47.9 %shard_map.117 = (bf16[64,64,128]{2,1,0:T(8,128)(2,1)S(1)}, bf16[64,64,128]{2,1,0:T(8,128)(2,1)S(1)}, bf16[4,64,128]{2,1,0:T(8,128)(2,1)S(1)}) custom-call(s32[20]{0:T(128)S(1)} %concatenate.12.scalars, bf16[128,64,128]{2,1,0:T(8,128)(2,1)S(1)} %shard_map.116.prod_ref, bf16[64,256,128]{2,1,0:T(8,128)(2,1)} %collective-permute-done.2.x_ref.xm_ref.xp_ref, ...), custom_call_target="tpu_custom_call" | custom-call | flops 1879048192 | bytes 6291456 | tf_op jit(solution)/shard_map/pallas_call | solution.py:269
  443.9 23.7 %shard_map.120 = (bf16[32,64,128]{2,1,0:T(8,128)(2,1)S(1)}, bf16[32,64,128]{2,1,0:T(8,128)(2,1)S(1)}, bf16[4,32,128]{2,1,0:T(8,128)(2,1)S(1)}) custom-call(s32[20]{0:T(128)S(1)} %concatenate.12.scalars, bf16[128,32,128]{2,1,0:T(8,128)(2,1)S(1)} %shard_map.119.prod_ref, bf16[32,256,128]{2,1,0:T(8,128)(2,1)S(1)} %collective-permute-done.3.x_ref.xm_ref.xp_ref, ...), custom_call_target="tpu_custom_call" | custom-call | flops 939524096 | bytes 3145728 | tf_op jit(solution)/shard_map/pallas_call | solution.py:269
  468.3 24.6 %shard_map.123 = (bf16[32,64,128]{2,1,0:T(8,128)(2,1)S(1)}, bf16[32,64,128]{2,1,0:T(8,128)(2,1)S(1)}, bf16[4,32,128]{2,1,0:T(8,128)(2,1)S(1)}) custom-call(s32[20]{0:T(128)S(1)} %concatenate.12.scalars, bf16[128,32,128]{2,1,0:T(8,128)(2,1)S(1)} %shard_map.122.prod_ref, bf16[32,256,128]{2,1,0:T(8,128)(2,1)} %collective-permute-done.4.x_ref.xm_ref.xp_ref, ...), custom_call_target="tpu_custom_call" | custom-call | flops 939524096 | bytes 3145728 | tf_op jit(solution)/shard_map/pallas_call | solution.py:269
  495.2 1.4 collective-permute-start.6
  503.3 52.0 %collective-permute-done.5 = bf16[4,256,128]{2,1,0:T(8,128)(2,1)S(1)} collective-permute-done((bf16[4,256,128]{2,1,0:T(8,128)(2,1)}, bf16[4,256,128]{2,1,0:T(8,128)(2,1)S(1)}, u32[]{:S(2)}, u32[]{:S(2)}) %collective-permute-start.5) | collective-permute-done | bytes 262176 | tf_op jit(solution)/shard_map/ppermute | solution.py:456
  556.6 26.8 %collective-permute-done.7 = bf16[4,256,128]{2,1,0:T(8,128)(2,1)S(1)} collective-permute-done((bf16[4,256,128]{2,1,0:T(8,128)(2,1)}, bf16[4,256,128]{2,1,0:T(8,128)(2,1)S(1)}, u32[]{:S(2)}, u32[]{:S(2)}) %collective-permute-start.7) | collective-permute-done | bytes 262176 | tf_op jit(solution)/shard_map/ppermute | solution.py:456
  588.1 6.7 collective-permute-done.11.refs_8_
  594.8 8.9 %collective-permute-done.12.refs_9_ = bf16[32,64,128]{2,1,0:T(8,128)(2,1)} collective-permute-done((bf16[32,64,128]{2,1,0:T(8,128)(2,1)}, bf16[32,64,128]{2,1,0:T(8,128)(2,1)}, u32[]{:S(2)}, u32[]{:S(2)}) %collective-permute-start.12) | collective-permute-done | bytes 524320 | tf_op jit(solution)/shard_map/ppermute | solution.py:456
  608.2 29.1 %shard_map.124 = (bf16[64,16,128]{2,1,0:T(8,128)(2,1)S(1)}, bf16[64,16,128]{2,1,0:T(8,128)(2,1)S(1)}, bf16[64,16,128]{2,1,0:T(8,128)(2,1)S(1)}, bf16[64,16,128]{2,1,0:T(8,128)(2,1)S(1)}) custom-call(s32[20]{0:T(128)S(1)} %concatenate.12.scalars, bf16[4,256,128]{2,1,0:T(8,128)(2,1)S(1)} %broadcast_select_fusion.1.bias_own_ref, ...), custom_call_target="tpu_custom_call" | custom-call | flops 3087007744 | bytes 3145728 | tf_op jit(solution)/shard_map/pallas_call | solution.py:393
  637.4 3.0 collective-permute-start.14
  641.2 29.0 %shard_map.125 = (bf16[64,16,128]{2,1,0:T(8,128)(2,1)S(1)}, bf16[64,16,128]{2,1,0:T(8,128)(2,1)S(1)}, bf16[64,16,128]{2,1,0:T(8,128)(2,1)S(1)}, bf16[64,16,128]{2,1,0:T(8,128)(2,1)S(1)}) custom-call(s32[20]{0:T(128)S(1)} %concatenate.12.scalars, bf16[4,256,128]{2,1,0:T(8,128)(2,1)S(1)} %broadcast_select_fusion.1.bias_own_ref, ...), custom_call_target="tpu_custom_call" | custom-call | flops 3087007744 | bytes 3145728 | tf_op jit(solution)/shard_map/pallas_call | solution.py:393
  672.4 29.0 %shard_map.126 = (bf16[64,16,128]{2,1,0:T(8,128)(2,1)S(1)}, bf16[64,16,128]{2,1,0:T(8,128)(2,1)S(1)}, bf16[64,16,128]{2,1,0:T(8,128)(2,1)S(1)}, bf16[64,16,128]{2,1,0:T(8,128)(2,1)S(1)}) custom-call(s32[20]{0:T(128)S(1)} %concatenate.12.scalars, bf16[4,256,128]{2,1,0:T(8,128)(2,1)S(1)} %broadcast_select_fusion.1.bias_own_ref, ...), custom_call_target="tpu_custom_call" | custom-call | flops 3087007744 | bytes 3145728 | tf_op jit(solution)/shard_map/pallas_call | solution.py:393
  701.4 29.0 %shard_map.127 = (bf16[64,16,128]{2,1,0:T(8,128)(2,1)S(1)}, bf16[64,16,128]{2,1,0:T(8,128)(2,1)S(1)}, bf16[64,16,128]{2,1,0:T(8,128)(2,1)S(1)}, bf16[64,16,128]{2,1,0:T(8,128)(2,1)S(1)}) custom-call(s32[20]{0:T(128)S(1)} %concatenate.12.scalars, bf16[4,256,128]{2,1,0:T(8,128)(2,1)S(1)} %broadcast_select_fusion.1.bias_own_ref, ...), custom_call_target="tpu_custom_call" | custom-call | flops 3087007744 | bytes 3145728 | tf_op jit(solution)/shard_map/pallas_call | solution.py:393
  731.4 2.9 collective-permute-start.18
  735.9 2.6 collective-permute-start.21
  739.3 9.1 %collective-permute-done.18 = bf16[64,16,128]{2,1,0:T(8,128)(2,1)S(1)} collective-permute-done((bf16[64,16,128]{2,1,0:T(8,128)(2,1)S(1)}, bf16[64,16,128]{2,1,0:T(8,128)(2,1)S(1)}, u32[]{:S(2)}, u32[]{:S(2)}) %collective-permute-start.18) | collective-permute-done | bytes 262176 | tf_op jit(solution)/shard_map/ppermute | solution.py:456
  749.6 7.2 collective-permute-start.24
  756.9 11.9 %collective-permute-done.20 = bf16[64,16,128]{2,1,0:T(8,128)(2,1)S(1)} collective-permute-done((bf16[64,16,128]{2,1,0:T(8,128)(2,1)S(1)}, bf16[64,16,128]{2,1,0:T(8,128)(2,1)S(1)}, u32[]{:S(2)}, u32[]{:S(2)}) %collective-permute-start.20) | collective-permute-done | bytes 262176 | tf_op jit(solution)/shard_map/ppermute | solution.py:456
  769.0 11.0 %collective-permute-done.23 = bf16[64,16,128]{2,1,0:T(8,128)(2,1)S(1)} collective-permute-done((bf16[64,16,128]{2,1,0:T(8,128)(2,1)S(1)}, bf16[64,16,128]{2,1,0:T(8,128)(2,1)S(1)}, u32[]{:S(2)}, u32[]{:S(2)}) %collective-permute-start.23) | collective-permute-done | bytes 262176 | tf_op jit(solution)/shard_map/ppermute | solution.py:456
  780.1 2.0 copy-done.27
  (143 shorter events, 38.1 us)
Async XLA Ops:
  0.0 17.8 %copy-start.32 = (bf16[128,128]{1,0:T(8,128)(2,1)S(1)}, bf16[128,128]{1,0:T(8,128)(2,1)}, u32[]{:S(2)}) copy-start(bf16[128,128]{1,0:T(8,128)(2,1)} %param.19) | copy-start | bytes 98308
  0.0 17.8 %copy-start.33 = (bf16[128,128]{1,0:T(8,128)(2,1)S(1)}, bf16[128,128]{1,0:T(8,128)(2,1)}, u32[]{:S(2)}) copy-start(bf16[128,128]{1,0:T(8,128)(2,1)} %param.17) | copy-start | bytes 98308
  0.0 56.5 %copy-start.31 = (bf16[4,128,128]{2,1,0:T(8,128)(2,1)S(1)}, bf16[4,128,128]{2,1,0:T(8,128)(2,1)}, u32[]{:S(2)}) copy-start(bf16[4,128,128]{2,1,0:T(8,128)(2,1)} %param.16) | copy-start | bytes 393220
  0.0 101.6 %copy-start.36 = (f32[128]{0:T(128)S(1)}, f32[128]{0:T(128)}, u32[]{:S(2)}) copy-start(f32[128]{0:T(128)} %param.18) | copy-start | bytes 1540
  0.0 101.8 %copy-start.35 = (bf16[128,4]{0,1:T(4,128)(2,1)S(1)}, bf16[128,4]{0,1:T(4,128)(2,1)}, u32[]{:S(2)}) copy-start(bf16[128,4]{0,1:T(4,128)(2,1)} %param.22) | copy-start | bytes 3076
  0.0 104.5 %copy-start.9 = (f32[128]{0:T(128)S(1)}, f32[128]{0:T(128)}, u32[]{:S(2)}) copy-start(f32[128]{0:T(128)} %param.15) | copy-start | bytes 1540
  4.0 51.0 %collective-permute-start = (bf16[32,256,128]{2,1,0:T(8,128)(2,1)S(1)}, bf16[32,256,128]{2,1,0:T(8,128)(2,1)}, u32[]{:S(2)}, u32[]{:S(2)}) collective-permute-start(bf16[32,256,128]{2,1,0:T(8,128)(2,1)S(1)} %get-tuple-element.98), channel_id=1, source_target_pairs={{0,4},{12,8},{1,5},{13,9},{2,6},{14,10},{3,7},{15,11},{16,20},{28,... | collective-permute-start | bytes 6291464 | tf_op jit(solution)/shard_map/ppermute | solution.py:456
  10.3 322.3 %collective-permute-start.2 = (bf16[64,256,128]{2,1,0:T(8,128)(2,1)}, bf16[64,256,128]{2,1,0:T(8,128)(2,1)}, u32[]{:S(2)}, u32[]{:S(2)}) collective-permute-start(bf16[64,256,128]{2,1,0:T(8,128)(2,1)} %bitcast.9.x_ref.xm_ref.xp_ref), channel_id=1, source_target_pairs={{4,8},{8,4},{5,9},{9,5},{6,10},{10,6},{7,11},{11,7},{20,24},{24,20... | collective-permute-start | bytes 12582920 | tf_op jit(solution)/shard_map/ppermute | solution.py:456
  12.9 86.0 %collective-permute-start.1 = (bf16[32,256,128]{2,1,0:T(8,128)(2,1)}, bf16[32,256,128]{2,1,0:T(8,128)(2,1)}, u32[]{:S(2)}, u32[]{:S(2)}) collective-permute-start(bf16[32,256,128]{2,1,0:T(8,128)(2,1)} %get-tuple-element.97), channel_id=1, source_target_pairs={{0,4},{12,8},{1,5},{13,9},{2,6},{14,10},{3,7},{15,11},{16,20},{28,... | collective-permute-start | bytes 6291464 | tf_op jit(solution)/shard_map/ppermute | solution.py:456
  55.0 257.9 %collective-permute-start.3 = (bf16[32,256,128]{2,1,0:T(8,128)(2,1)}, bf16[32,256,128]{2,1,0:T(8,128)(2,1)S(1)}, u32[]{:S(2)}, u32[]{:S(2)}) collective-permute-start(bf16[32,256,128]{2,1,0:T(8,128)(2,1)} %collective-permute-done), channel_id=1, source_target_pairs={{4,8},{8,4},{5,9},{9,5},{6,10},{10,6},{7,11},{11,7},{20,24},{24,20... | collective-permute-start | bytes 6291464 | tf_op jit(solution)/shard_map/ppermute | solution.py:456
  98.9 275.2 %collective-permute-start.4 = (bf16[32,256,128]{2,1,0:T(8,128)(2,1)}, bf16[32,256,128]{2,1,0:T(8,128)(2,1)}, u32[]{:S(2)}, u32[]{:S(2)}) collective-permute-start(bf16[32,256,128]{2,1,0:T(8,128)(2,1)} %collective-permute-done.1), channel_id=1, source_target_pairs={{4,8},{8,4},{5,9},{9,5},{6,10},{10,6},{7,11},{11,7},{20,24},{24,20... | collective-permute-start | bytes 6291464 | tf_op jit(solution)/shard_map/ppermute | solution.py:456
  140.9 2.0 copy-start.5
  181.9 2.0 copy-start
  185.9 2.2 copy-start.6
  200.0 2.2 copy-start.8
  202.2 10.6 %copy-start.10 = (f32[128]{0:T(128)S(1)}, f32[128]{0:T(128)}, u32[]{:S(2)}) copy-start(f32[128]{0:T(128)} %param.20) | copy-start | bytes 1540
  311.9 16.2 %copy-start.1 = (bf16[128,64,256]{2,1,0:T(8,128)(2,1)S(1)}, bf16[128,64,256]{2,1,0:T(8,128)(2,1)}, u32[]{:S(2)}) copy-start(bf16[128,64,256]{2,1,0:T(8,128)(2,1)} %copy-done) | copy-start | bytes 12582916
  374.1 16.7 %copy-start.2 = (bf16[128,64,256]{2,1,0:T(8,128)(2,1)S(1)}, bf16[128,64,256]{2,1,0:T(8,128)(2,1)}, u32[]{:S(2)}) copy-start(bf16[128,64,256]{2,1,0:T(8,128)(2,1)} %copy-done) | copy-start | bytes 12582916
  443.2 49.8 %copy-start.13 = (bf16[64,64,128]{2,1,0:T(8,128)(2,1)}, bf16[64,64,128]{2,1,0:T(8,128)(2,1)S(1)}, u32[]{:S(2)}) copy-start(bf16[64,64,128]{2,1,0:T(8,128)(2,1)S(1)} %get-tuple-element.71.refs_2_) | copy-start | bytes 3145732
  443.2 52.0 %copy-start.19 = (bf16[64,64,128]{2,1,0:T(8,128)(2,1)}, bf16[64,64,128]{2,1,0:T(8,128)(2,1)S(1)}, u32[]{:S(2)}) copy-start(bf16[64,64,128]{2,1,0:T(8,128)(2,1)S(1)} %get-tuple-element.76) | copy-start | bytes 3145732
  467.6 27.6 %copy-start.20 = (bf16[32,64,128]{2,1,0:T(8,128)(2,1)}, bf16[32,64,128]{2,1,0:T(8,128)(2,1)S(1)}, u32[]{:S(2)}) copy-start(bf16[32,64,128]{2,1,0:T(8,128)(2,1)S(1)} %get-tuple-element.72.refs_3_) | copy-start | bytes 1572868
  467.6 27.6 %copy-start.25 = (bf16[32,64,128]{2,1,0:T(8,128)(2,1)}, bf16[32,64,128]{2,1,0:T(8,128)(2,1)S(1)}, u32[]{:S(2)}) copy-start(bf16[32,64,128]{2,1,0:T(8,128)(2,1)S(1)} %get-tuple-element.77) | copy-start | bytes 1572868
  467.6 29.0 %copy-start.30 = (bf16[4,128,128]{2,1,0:T(8,128)(2,1)S(1)}, bf16[4,128,128]{2,1,0:T(8,128)(2,1)}, u32[]{:S(2)}) copy-start(bf16[4,128,128]{2,1,0:T(8,128)(2,1)} %param.21) | copy-start | bytes 393220
  467.7 117.2 %copy-start.34 = (bf16[128,128]{1,0:T(8,128)(2,1)S(1)}, bf16[128,128]{1,0:T(8,128)(2,1)}, u32[]{:S(2)}) copy-start(bf16[128,128]{1,0:T(8,128)(2,1)} %param.23) | copy-start | bytes 98308
  467.7 136.0 %copy-start.12 = (bf16[64,64,128]{2,1,0:T(8,128)(2,1)S(1)}, bf16[64,64,128]{2,1,0:T(8,128)(2,1)}, u32[]{:S(2)}) copy-start(bf16[64,64,128]{2,1,0:T(8,128)(2,1)} %copy-done.11) | copy-start | bytes 3145732
  495.2 6.7 collective-permute-start.6
  496.8 90.3 %collective-permute-start.8 = (bf16[64,64,128]{2,1,0:T(8,128)(2,1)}, bf16[64,64,128]{2,1,0:T(8,128)(2,1)S(1)}, u32[]{:S(2)}, u32[]{:S(2)}) collective-permute-start(bf16[64,64,128]{2,1,0:T(8,128)(2,1)} %copy-done.15), channel_id=1, source_target_pairs={{4,0},{8,12},{5,1},{9,13},{6,2},{10,14},{7,3},{11,15},{20,16},{24,... | collective-permute-start | bytes 3145736 | tf_op jit(solution)/shard_map/ppermute | solution.py:456
  498.1 90.0 %collective-permute-start.9 = (bf16[64,64,128]{2,1,0:T(8,128)(2,1)}, bf16[64,64,128]{2,1,0:T(8,128)(2,1)}, u32[]{:S(2)}, u32[]{:S(2)}) collective-permute-start(bf16[64,64,128]{2,1,0:T(8,128)(2,1)} %copy-done.16), channel_id=1, source_target_pairs={{4,0},{8,12},{5,1},{9,13},{6,2},{10,14},{7,3},{11,15},{20,16},{24,... | collective-permute-start | bytes 3145736 | tf_op jit(solution)/shard_map/ppermute | solution.py:456
  499.4 56.0 %collective-permute-start.5 = (bf16[4,256,128]{2,1,0:T(8,128)(2,1)}, bf16[4,256,128]{2,1,0:T(8,128)(2,1)S(1)}, u32[]{:S(2)}, u32[]{:S(2)}) collective-permute-start(bf16[4,256,128]{2,1,0:T(8,128)(2,1)} %constant_dynamic-update-slice_fusion.2), channel_id=1, source_target_pairs={{4,0},{8,12},{5,1},{9,13},{6,2},{10,14},{7,3},{11,15},{20,16},{24,... | collective-permute-start | bytes 786440 | tf_op jit(solution)/shard_map/ppermute | solution.py:456
  500.7 103.0 %collective-permute-start.10 = (bf16[64,64,128]{2,1,0:T(8,128)(2,1)}, bf16[64,64,128]{2,1,0:T(8,128)(2,1)}, u32[]{:S(2)}, u32[]{:S(2)}) collective-permute-start(bf16[64,64,128]{2,1,0:T(8,128)(2,1)} %copy-done.19), channel_id=1, source_target_pairs={{4,0},{8,12},{5,1},{9,13},{6,2},{10,14},{7,3},{11,15},{20,16},{24,... | collective-permute-start | bytes 3145736 | tf_op jit(solution)/shard_map/ppermute | solution.py:456
  502.0 81.5 %collective-permute-start.7 = (bf16[4,256,128]{2,1,0:T(8,128)(2,1)}, bf16[4,256,128]{2,1,0:T(8,128)(2,1)S(1)}, u32[]{:S(2)}, u32[]{:S(2)}) collective-permute-start(bf16[4,256,128]{2,1,0:T(8,128)(2,1)} %collective-permute-done.6), channel_id=1, source_target_pairs={{4,0},{8,12},{5,1},{9,13},{6,2},{10,14},{7,3},{11,15},{20,16},{24,... | collective-permute-start | bytes 786440 | tf_op jit(solution)/shard_map/ppermute | solution.py:456
  555.3 29.4 %copy-start.28 = (bf16[4,256,128]{2,1,0:T(8,128)(2,1)}, bf16[4,256,128]{2,1,0:T(8,128)(2,1)S(1)}, u32[]{:S(2)}) copy-start(bf16[4,256,128]{2,1,0:T(8,128)(2,1)S(1)} %collective-permute-done.5) | copy-start | bytes 786436
  555.4 39.4 %collective-permute-start.11 = (bf16[32,64,128]{2,1,0:T(8,128)(2,1)}, bf16[32,64,128]{2,1,0:T(8,128)(2,1)}, u32[]{:S(2)}, u32[]{:S(2)}) collective-permute-start(bf16[32,64,128]{2,1,0:T(8,128)(2,1)} %copy-done.25), channel_id=1, source_target_pairs={{4,0},{8,12},{5,1},{9,13},{6,2},{10,14},{7,3},{11,15},{20,16},{24,... | collective-permute-start | bytes 1572872 | tf_op jit(solution)/shard_map/ppermute | solution.py:456
  583.4 20.2 %collective-permute-start.12 = (bf16[32,64,128]{2,1,0:T(8,128)(2,1)}, bf16[32,64,128]{2,1,0:T(8,128)(2,1)}, u32[]{:S(2)}, u32[]{:S(2)}) collective-permute-start(bf16[32,64,128]{2,1,0:T(8,128)(2,1)} %copy-done.26), channel_id=1, source_target_pairs={{4,0},{8,12},{5,1},{9,13},{6,2},{10,14},{7,3},{11,15},{20,16},{24,... | collective-permute-start | bytes 1572872 | tf_op jit(solution)/shard_map/ppermute | solution.py:456
  608.2 33.0 %copy-start.22 = (bf16[32,64,128]{2,1,0:T(8,128)(2,1)S(1)}, bf16[32,64,128]{2,1,0:T(8,128)(2,1)}, u32[]{:S(2)}) copy-start(bf16[32,64,128]{2,1,0:T(8,128)(2,1)} %copy-done.20) | copy-start | bytes 1572868
  637.4 94.0 %collective-permute-start.13 = (bf16[64,16,128]{2,1,0:T(8,128)(2,1)S(1)}, bf16[64,16,128]{2,1,0:T(8,128)(2,1)S(1)}, u32[]{:S(2)}, u32[]{:S(2)}) collective-permute-start(bf16[64,16,128]{2,1,0:T(8,128)(2,1)S(1)} %get-tuple-element.80), channel_id=1, source_target_pairs={{0,4},{4,8},{8,12},{12,0},{1,5},{5,9},{9,13},{13,1},{2,6},{6,10},{... | collective-permute-start | bytes 786440 | tf_op jit(solution)/shard_map/ppermute | solution.py:456
  637.4 96.9 %collective-permute-start.14 = (bf16[64,16,128]{2,1,0:T(8,128)(2,1)S(1)}, bf16[64,16,128]{2,1,0:T(8,128)(2,1)S(1)}, u32[]{:S(2)}, u32[]{:S(2)}) collective-permute-start(bf16[64,16,128]{2,1,0:T(8,128)(2,1)S(1)} %get-tuple-element.81), channel_id=1, source_target_pairs={{0,8},{4,12},{8,0},{12,4},{1,9},{5,13},{9,1},{13,5},{2,10},{6,14},... | collective-permute-start | bytes 786440 | tf_op jit(solution)/shard_map/ppermute | solution.py:456
  640.5 94.0 %collective-permute-start.15 = (bf16[64,16,128]{2,1,0:T(8,128)(2,1)S(1)}, bf16[64,16,128]{2,1,0:T(8,128)(2,1)S(1)}, u32[]{:S(2)}, u32[]{:S(2)}) collective-permute-start(bf16[64,16,128]{2,1,0:T(8,128)(2,1)S(1)} %get-tuple-element.82), channel_id=1, source_target_pairs={{0,12},{4,0},{8,4},{12,8},{1,13},{5,1},{9,5},{13,9},{2,14},{6,2},{... | collective-permute-start | bytes 786440 | tf_op jit(solution)/shard_map/ppermute | solution.py:456
  670.2 65.7 %collective-permute-start.16 = (bf16[64,16,128]{2,1,0:T(8,128)(2,1)S(1)}, bf16[64,16,128]{2,1,0:T(8,128)(2,1)S(1)}, u32[]{:S(2)}, u32[]{:S(2)}) collective-permute-start(bf16[64,16,128]{2,1,0:T(8,128)(2,1)S(1)} %get-tuple-element.84), channel_id=1, source_target_pairs={{0,4},{4,8},{8,12},{12,0},{1,5},{5,9},{9,13},{13,1},{2,6},{6,10},{... | collective-permute-start | bytes 786440 | tf_op jit(solution)/shard_map/ppermute | solution.py:456
  671.5 67.1 %collective-permute-start.17 = (bf16[64,16,128]{2,1,0:T(8,128)(2,1)S(1)}, bf16[64,16,128]{2,1,0:T(8,128)(2,1)S(1)}, u32[]{:S(2)}, u32[]{:S(2)}) collective-permute-start(bf16[64,16,128]{2,1,0:T(8,128)(2,1)S(1)} %get-tuple-element.85), channel_id=1, source_target_pairs={{0,8},{4,12},{8,0},{12,4},{1,9},{5,13},{9,1},{13,5},{2,10},{6,14},... | collective-permute-start | bytes 786440 | tf_op jit(solution)/shard_map/ppermute | solution.py:456
  731.4 17.0 %collective-permute-start.18 = (bf16[64,16,128]{2,1,0:T(8,128)(2,1)S(1)}, bf16[64,16,128]{2,1,0:T(8,128)(2,1)S(1)}, u32[]{:S(2)}, u32[]{:S(2)}) collective-permute-start(bf16[64,16,128]{2,1,0:T(8,128)(2,1)S(1)} %get-tuple-element.86), channel_id=1, source_target_pairs={{0,12},{4,0},{8,4},{12,8},{1,13},{5,1},{9,5},{13,9},{2,14},{6,2},{... | collective-permute-start | bytes 786440 | tf_op jit(solution)/shard_map/ppermute | solution.py:456
  734.4 15.2 %collective-permute-start.19 = (bf16[64,16,128]{2,1,0:T(8,128)(2,1)S(1)}, bf16[64,16,128]{2,1,0:T(8,128)(2,1)S(1)}, u32[]{:S(2)}, u32[]{:S(2)}) collective-permute-start(bf16[64,16,128]{2,1,0:T(8,128)(2,1)S(1)} %get-tuple-element.88), channel_id=1, source_target_pairs={{0,4},{4,8},{8,12},{12,0},{1,5},{5,9},{9,13},{13,1},{2,6},{6,10},{... | collective-permute-start | bytes 786440 | tf_op jit(solution)/shard_map/ppermute | solution.py:456
  734.5 34.3 %collective-permute-start.20 = (bf16[64,16,128]{2,1,0:T(8,128)(2,1)S(1)}, bf16[64,16,128]{2,1,0:T(8,128)(2,1)S(1)}, u32[]{:S(2)}, u32[]{:S(2)}) collective-permute-start(bf16[64,16,128]{2,1,0:T(8,128)(2,1)S(1)} %get-tuple-element.89), channel_id=1, source_target_pairs={{0,8},{4,12},{8,0},{12,4},{1,9},{5,13},{9,1},{13,5},{2,10},{6,14},... | collective-permute-start | bytes 786440 | tf_op jit(solution)/shard_map/ppermute | solution.py:456
  735.9 32.9 %collective-permute-start.21 = (bf16[64,16,128]{2,1,0:T(8,128)(2,1)S(1)}, bf16[64,16,128]{2,1,0:T(8,128)(2,1)S(1)}, u32[]{:S(2)}, u32[]{:S(2)}) collective-permute-start(bf16[64,16,128]{2,1,0:T(8,128)(2,1)S(1)} %get-tuple-element.90), channel_id=1, source_target_pairs={{0,12},{4,0},{8,4},{12,8},{1,13},{5,1},{9,5},{13,9},{2,14},{6,2},{... | collective-permute-start | bytes 786440 | tf_op jit(solution)/shard_map/ppermute | solution.py:456
  738.6 30.4 %collective-permute-start.22 = (bf16[64,16,128]{2,1,0:T(8,128)(2,1)S(1)}, bf16[64,16,128]{2,1,0:T(8,128)(2,1)S(1)}, u32[]{:S(2)}, u32[]{:S(2)}) collective-permute-start(bf16[64,16,128]{2,1,0:T(8,128)(2,1)S(1)} %get-tuple-element.92), channel_id=1, source_target_pairs={{0,4},{4,8},{8,12},{12,0},{1,5},{5,9},{9,13},{13,1},{2,6},{6,10},{... | collective-permute-start | bytes 786440 | tf_op jit(solution)/shard_map/ppermute | solution.py:456
  748.4 31.7 %collective-permute-start.23 = (bf16[64,16,128]{2,1,0:T(8,128)(2,1)S(1)}, bf16[64,16,128]{2,1,0:T(8,128)(2,1)S(1)}, u32[]{:S(2)}, u32[]{:S(2)}) collective-permute-start(bf16[64,16,128]{2,1,0:T(8,128)(2,1)S(1)} %get-tuple-element.93), channel_id=1, source_target_pairs={{0,8},{4,12},{8,0},{12,4},{1,9},{5,13},{9,1},{13,5},{2,10},{6,14},... | collective-permute-start | bytes 786440 | tf_op jit(solution)/shard_map/ppermute | solution.py:456
  749.6 30.5 %collective-permute-start.24 = (bf16[64,16,128]{2,1,0:T(8,128)(2,1)S(1)}, bf16[64,16,128]{2,1,0:T(8,128)(2,1)S(1)}, u32[]{:S(2)}, u32[]{:S(2)}) collective-permute-start(bf16[64,16,128]{2,1,0:T(8,128)(2,1)S(1)} %get-tuple-element.94), channel_id=1, source_target_pairs={{0,12},{4,0},{8,4},{12,8},{1,13},{5,1},{9,5},{13,9},{2,14},{6,2},{... | collective-permute-start | bytes 786440 | tf_op jit(solution)/shard_map/ppermute | solution.py:456
  780.1 2.0 copy-start.27
  (14 other events, 16.4 us)
